TPU v7x, 32 devices: a whole 2x2x4 slice. The times are simulated.
32 devices in a mesh: grp: 2 (over x), seq: 16 (over z, y, core).
Axes of the slice: x: 2, y: 2, z: 4, core: 2. Of those that a mesh axis runs over, the one named last changes fastest.
Arguments:
- layer_ids: int32 [2], P('grp'), parts along dimension 0, may hold values from 0 to 15
- seq_ids: int32 [128], P(('grp', 'seq')), parts along dimension 0, may hold values from 0 to 1
- out_eigen: float32 [16, 32768], P(None, 'seq'), as said below
- in_eigen: float32 [16, 8192], P(None, 'seq'), as said below
- query_out: float32 [1, 4, 32, 32768], P(None, 'grp', None, 'seq'), parts along dimension 1, may hold values from -6 to 6
- query_in: float32 [1, 4, 32, 8192], P(None, 'grp', None, 'seq'), parts along dimension 1, may hold values from -6 to 6
- train_out: float32 [1, 64, 32, 32768], P(None, ('grp', 'seq')), parts along dimension 1, may hold values from -2.4 to 2.4
- train_in: float32 [1, 64, 32, 8192], P(None, ('grp', 'seq')), parts along dimension 1, may hold values from -2.4 to 2.4
Outputs:
- influence: float32 [4, 64], P('grp', 'seq'), parts along dimension 0
There are 2 independent parts, one for each index of `grp`. A program takes and returns all parts, laid end to end along the dimension named above; an argument that names none is the same for every part. Nothing has to cross between parts.
Inputs may be any that keep to these rules, and one draw needn't show every extreme that they name: `out_eigen`: every entry is positive. `in_eigen`: every entry is positive.
All inputs are finite; a program needn't handle non-finite values.
Results may differ from a plain program's by a relative error of at most 0.00015.
Values sent between devices are 32-bit elements; how exact they have to be, the bound alone decides.
A program may use at most 64 MiB of HBM per device.

v0:
```python
import jax
import jax.numpy as jnp
from jax import lax
from jax.sharding import PartitionSpec as P

damping = 0.1
epsilon = 1e-06


def passed_along(shard, axis, by):
    devices = lax.axis_size(axis)
    return lax.ppermute(shard, axis, [(i, (i + by) % devices) for i in range(devices)])


def pick_layers(stored_values, layer_ids):
    one_hot = (
        layer_ids[:, None] == jnp.arange(stored_values.shape[0], dtype=jnp.int32)[None, :]
    ).astype(jnp.float32)
    return jnp.sum(one_hot[:, :, None] * stored_values[None, :, :], axis=1)


def contract(factors, others):
    return jnp.einsum("lqri,ltsi->lqrts", factors, others, precision=lax.Precision.HIGHEST)


def self_gram(factors):
    return jnp.einsum("lqri,lqsi->lqrs", factors, factors, precision=lax.Precision.HIGHEST)


def local(layer_ids, seq_ids, out_eigen, in_eigen, query_out, query_in, train_out, train_in):
    scaled_out = query_out / (pick_layers(out_eigen, layer_ids)[:, None, None, :] + damping)
    scaled_in = query_in / (pick_layers(in_eigen, layer_ids)[:, None, None, :] + damping)
    out_cols = scaled_out.shape[3]
    in_cols = scaled_in.shape[3]
    joined = jnp.concatenate([scaled_out, scaled_in], axis=3)

    def absorb(totals, block_out, block_in, first_shard):
        count_out = block_out.shape[3]
        count_in = block_in.shape[3]
        train_cols_out = lax.dynamic_slice_in_dim(train_out, first_shard * out_cols, count_out, 3)
        train_cols_in = lax.dynamic_slice_in_dim(train_in, first_shard * in_cols, count_in, 3)
        acc_out = totals[0] + contract(block_out, train_cols_out)
        acc_in = totals[1] + contract(block_in, train_cols_in)
        return (acc_out, acc_in, totals[2], totals[3])

    sampled, queries, rank = (scaled_out.shape[0], scaled_out.shape[1], scaled_out.shape[2])
    pool = train_out.shape[1]
    cross_zero = jnp.zeros((sampled, queries, rank, pool, rank), jnp.float32)
    gram_zero = jnp.zeros((sampled, queries, rank, rank), jnp.float32)
    initial = (cross_zero, cross_zero, gram_zero, gram_zero)
    loop_size = lax.axis_size("seq")
    position = lax.axis_index("seq")

    def turn(turn_index, carried):
        totals, moving = carried
        anchor = (position - turn_index) % loop_size
        totals = absorb(totals, moving[..., :out_cols], moving[..., out_cols:], anchor)
        moving = passed_along(moving, "seq", 1)
        return (totals, moving)

    totals, moving = lax.fori_loop(0, loop_size - 1, turn, (initial, joined))
    anchor = (position - (loop_size - 1)) % loop_size
    totals = absorb(totals, moving[..., :out_cols], moving[..., out_cols:], anchor)
    cross_out, cross_in = (totals[0], totals[1])
    gram_out, gram_in = lax.psum((self_gram(scaled_out), self_gram(scaled_in)), "seq")
    query_norm = jnp.sum(gram_out * gram_in, axis=(0, 2, 3))
    unscaled = jnp.sum(cross_out * cross_in, axis=(0, 2, 4))
    one_hot = (seq_ids[:, None] == jnp.arange(pool, dtype=jnp.int32)[None, :]).astype(jnp.float32)
    picked = jnp.sum(unscaled[:, None, :] * one_hot[None, :, :], axis=2)
    return picked / jnp.sqrt(query_norm + epsilon)[:, None]


def solution(mesh):
    in_specs = (
        P("grp"),
        P(("grp", "seq")),
        P(None, "seq"),
        P(None, "seq"),
        P(None, "grp", None, "seq"),
        P(None, "grp", None, "seq"),
        P(None, ("grp", "seq"), None, None),
        P(None, ("grp", "seq"), None, None),
    )
    out_specs = P("grp", "seq")
    return jax.shard_map(local, mesh=mesh, in_specs=in_specs, out_specs=out_specs, check_vma=False)
```

profile of v0, /device:TPU:0, one launch (start us, length us, event | category | flops | bytes accessed | tf_op | source)
XLA Modules:
  0.0 266.2 jit_solution(3210098148694948976)
XLA Ops:
  0.7 0.7 compare_convert_fusion
  1.3 0.8 multiply_reduce_fusion.2
  2.2 1.0 multiply_reduce_fusion
  3.2 0.9 broadcast_divide_fusion.1
  4.1 0.2 convolution_bitcast_fusion.4
  4.4 1.1 broadcast_divide_fusion
  5.5 0.6 convolution_bitcast_fusion.5
  6.1 63.1 %all-reduce = (f32[1,2,32,32]{3,2,1,0:T(8,128)S(1)}, f32[1,2,32,32]{3,2,1,0:T(8,128)S(1)}) all-reduce(f32[1,2,32,32]{3,2,1,0:T(8,128)S(1)} %convolution_bitcast_fusion.5, f32[1,2,32,32]{3,2,1,0:T(8,128)S(1)} %convolution_bitcast_fusion.4), channel_id=1, replica_groups=mesh['grp'=2,'seq'=16] {'seq'}, use_global_device_ids=true, to_apply=%region_6.7 | all-reduce | flops 4096 | bytes 32768 | tf_op jit(solution)/shard_map/psum | solution.py:65
  69.2 0.1 multiply_reduce_fusion.1
  69.3 192.1 %while.20 = (s32[]{:T(128)}, f32[1,2,32,2,32]{2,4,1,3,0:T(8,128)S(1)}, f32[1,2,32,2,32]{2,4,1,3,0:T(8,128)S(1)}, f32[1,2,32,2560]{3,2,1,0:T(8,128)S(1)}, s32[]{:...) while((s32[]{:T(128)}, ...), condition=%wide.region_3.4_spmd.clone, body=%wide.region_2.3_spmd.clone.sunk | while | flops 125845520 | bytes 5407133 | solution.py:61
  69.4 1.4 fusion.39
  70.8 2.5 fusion.38
  73.3 8.8 %collective-permute-done = f32[1,2,32,2560]{3,2,1,0:T(8,128)S(1)} collective-permute-done((f32[1,2,32,2560]{3,2,1,0:T(8,128)S(1)}, f32[1,2,32,2560]{3,2,1,0:T(8,128)S(1)}, u32[]{:S(2)}, u32[]{:S(2)}) %collective-permute-start) | collective-permute-done | bytes 655392 | tf_op jit(solution)/shard_map/while/body/eval_jaxpr/ppermute | solution.py:12
  82.1 0.1 collective-permute-start
  82.2 1.4 fusion.39
  83.6 2.5 fusion.38
  86.1 8.8 %collective-permute-done = f32[1,2,32,2560]{3,2,1,0:T(8,128)S(1)} collective-permute-done((f32[1,2,32,2560]{3,2,1,0:T(8,128)S(1)}, f32[1,2,32,2560]{3,2,1,0:T(8,128)S(1)}, u32[]{:S(2)}, u32[]{:S(2)}) %collective-permute-start) | collective-permute-done | bytes 655392 | tf_op jit(solution)/shard_map/while/body/eval_jaxpr/ppermute | solution.py:12
  94.9 0.1 collective-permute-start
  95.0 1.4 fusion.39
  96.4 2.5 fusion.38
  98.9 8.8 %collective-permute-done = f32[1,2,32,2560]{3,2,1,0:T(8,128)S(1)} collective-permute-done((f32[1,2,32,2560]{3,2,1,0:T(8,128)S(1)}, f32[1,2,32,2560]{3,2,1,0:T(8,128)S(1)}, u32[]{:S(2)}, u32[]{:S(2)}) %collective-permute-start) | collective-permute-done | bytes 655392 | tf_op jit(solution)/shard_map/while/body/eval_jaxpr/ppermute | solution.py:12
  107.8 0.1 collective-permute-start
  107.9 1.4 fusion.39
  109.2 2.5 fusion.38
  111.7 8.8 %collective-permute-done = f32[1,2,32,2560]{3,2,1,0:T(8,128)S(1)} collective-permute-done((f32[1,2,32,2560]{3,2,1,0:T(8,128)S(1)}, f32[1,2,32,2560]{3,2,1,0:T(8,128)S(1)}, u32[]{:S(2)}, u32[]{:S(2)}) %collective-permute-start) | collective-permute-done | bytes 655392 | tf_op jit(solution)/shard_map/while/body/eval_jaxpr/ppermute | solution.py:12
  120.7 1.4 fusion.39
  122.0 2.5 fusion.38
  124.5 8.8 %collective-permute-done = f32[1,2,32,2560]{3,2,1,0:T(8,128)S(1)} collective-permute-done((f32[1,2,32,2560]{3,2,1,0:T(8,128)S(1)}, f32[1,2,32,2560]{3,2,1,0:T(8,128)S(1)}, u32[]{:S(2)}, u32[]{:S(2)}) %collective-permute-start) | collective-permute-done | bytes 655392 | tf_op jit(solution)/shard_map/while/body/eval_jaxpr/ppermute | solution.py:12
  133.5 1.4 fusion.39
  134.9 2.5 fusion.38
  137.4 8.8 %collective-permute-done = f32[1,2,32,2560]{3,2,1,0:T(8,128)S(1)} collective-permute-done((f32[1,2,32,2560]{3,2,1,0:T(8,128)S(1)}, f32[1,2,32,2560]{3,2,1,0:T(8,128)S(1)}, u32[]{:S(2)}, u32[]{:S(2)}) %collective-permute-start) | collective-permute-done | bytes 655392 | tf_op jit(solution)/shard_map/while/body/eval_jaxpr/ppermute | solution.py:12
  146.3 1.4 fusion.39
  147.7 2.5 fusion.38
  150.2 8.8 %collective-permute-done = f32[1,2,32,2560]{3,2,1,0:T(8,128)S(1)} collective-permute-done((f32[1,2,32,2560]{3,2,1,0:T(8,128)S(1)}, f32[1,2,32,2560]{3,2,1,0:T(8,128)S(1)}, u32[]{:S(2)}, u32[]{:S(2)}) %collective-permute-start) | collective-permute-done | bytes 655392 | tf_op jit(solution)/shard_map/while/body/eval_jaxpr/ppermute | solution.py:12
  159.1 1.4 fusion.39
  160.5 2.5 fusion.38
  163.0 8.8 %collective-permute-done = f32[1,2,32,2560]{3,2,1,0:T(8,128)S(1)} collective-permute-done((f32[1,2,32,2560]{3,2,1,0:T(8,128)S(1)}, f32[1,2,32,2560]{3,2,1,0:T(8,128)S(1)}, u32[]{:S(2)}, u32[]{:S(2)}) %collective-permute-start) | collective-permute-done | bytes 655392 | tf_op jit(solution)/shard_map/while/body/eval_jaxpr/ppermute | solution.py:12
  171.9 1.4 fusion.39
  173.3 2.5 fusion.38
  175.8 8.8 %collective-permute-done = f32[1,2,32,2560]{3,2,1,0:T(8,128)S(1)} collective-permute-done((f32[1,2,32,2560]{3,2,1,0:T(8,128)S(1)}, f32[1,2,32,2560]{3,2,1,0:T(8,128)S(1)}, u32[]{:S(2)}, u32[]{:S(2)}) %collective-permute-start) | collective-permute-done | bytes 655392 | tf_op jit(solution)/shard_map/while/body/eval_jaxpr/ppermute | solution.py:12
  184.7 1.4 fusion.39
  186.1 2.5 fusion.38
  188.6 8.8 %collective-permute-done = f32[1,2,32,2560]{3,2,1,0:T(8,128)S(1)} collective-permute-done((f32[1,2,32,2560]{3,2,1,0:T(8,128)S(1)}, f32[1,2,32,2560]{3,2,1,0:T(8,128)S(1)}, u32[]{:S(2)}, u32[]{:S(2)}) %collective-permute-start) | collective-permute-done | bytes 655392 | tf_op jit(solution)/shard_map/while/body/eval_jaxpr/ppermute | solution.py:12
  197.5 1.4 fusion.39
  198.9 2.5 fusion.38
  201.4 8.8 %collective-permute-done = f32[1,2,32,2560]{3,2,1,0:T(8,128)S(1)} collective-permute-done((f32[1,2,32,2560]{3,2,1,0:T(8,128)S(1)}, f32[1,2,32,2560]{3,2,1,0:T(8,128)S(1)}, u32[]{:S(2)}, u32[]{:S(2)}) %collective-permute-start) | collective-permute-done | bytes 655392 | tf_op jit(solution)/shard_map/while/body/eval_jaxpr/ppermute | solution.py:12
  210.3 1.4 fusion.39
  211.7 2.5 fusion.38
  214.2 8.8 %collective-permute-done = f32[1,2,32,2560]{3,2,1,0:T(8,128)S(1)} collective-permute-done((f32[1,2,32,2560]{3,2,1,0:T(8,128)S(1)}, f32[1,2,32,2560]{3,2,1,0:T(8,128)S(1)}, u32[]{:S(2)}, u32[]{:S(2)}) %collective-permute-start) | collective-permute-done | bytes 655392 | tf_op jit(solution)/shard_map/while/body/eval_jaxpr/ppermute | solution.py:12
  223.1 1.4 fusion.39
  224.5 2.5 fusion.38
  227.0 8.8 %collective-permute-done = f32[1,2,32,2560]{3,2,1,0:T(8,128)S(1)} collective-permute-done((f32[1,2,32,2560]{3,2,1,0:T(8,128)S(1)}, f32[1,2,32,2560]{3,2,1,0:T(8,128)S(1)}, u32[]{:S(2)}, u32[]{:S(2)}) %collective-permute-start) | collective-permute-done | bytes 655392 | tf_op jit(solution)/shard_map/while/body/eval_jaxpr/ppermute | solution.py:12
  235.9 1.4 fusion.39
  237.3 2.5 fusion.38
  239.8 8.8 %collective-permute-done = f32[1,2,32,2560]{3,2,1,0:T(8,128)S(1)} collective-permute-done((f32[1,2,32,2560]{3,2,1,0:T(8,128)S(1)}, f32[1,2,32,2560]{3,2,1,0:T(8,128)S(1)}, u32[]{:S(2)}, u32[]{:S(2)}) %collective-permute-start) | collective-permute-done | bytes 655392 | tf_op jit(solution)/shard_map/while/body/eval_jaxpr/ppermute | solution.py:12
  248.7 1.4 fusion.39
  250.1 2.5 fusion.38
  252.6 8.8 %collective-permute-done = f32[1,2,32,2560]{3,2,1,0:T(8,128)S(1)} collective-permute-done((f32[1,2,32,2560]{3,2,1,0:T(8,128)S(1)}, f32[1,2,32,2560]{3,2,1,0:T(8,128)S(1)}, u32[]{:S(2)}, u32[]{:S(2)}) %collective-permute-start) | collective-permute-done | bytes 655392 | tf_op jit(solution)/shard_map/while/body/eval_jaxpr/ppermute | solution.py:12
  261.4 0.1 copy.11
  261.5 0.1 copy.12
  261.6 1.4 fusion.14
  262.9 2.6 fusion.15
  265.5 0.1 multiply_reduce_fusion.3
  265.6 0.6 broadcast_divide_fusion.2
  (34 shorter events, 1.4 us)
Async XLA Ops:
  69.3 12.8 %collective-permute-start = (f32[1,2,32,2560]{3,2,1,0:T(8,128)S(1)}, f32[1,2,32,2560]{3,2,1,0:T(8,128)S(1)}, u32[]{:S(2)}, u32[]{:S(2)}) collective-permute-start(f32[1,2,32,2560]{3,2,1,0:T(8,128)S(1)} %copy.24), channel_id=1, source_target_pairs={{0,1},{1,2},{2,3},{3,4},{4,5},{5,6},{6,7},{7,8},{8,9},{9,10},{10,1... | collective-permute-start | bytes 1966088 | tf_op jit(solution)/shard_map/while/body/eval_jaxpr/ppermute | solution.py:12
  82.1 12.8 %collective-permute-start = (f32[1,2,32,2560]{3,2,1,0:T(8,128)S(1)}, f32[1,2,32,2560]{3,2,1,0:T(8,128)S(1)}, u32[]{:S(2)}, u32[]{:S(2)}) collective-permute-start(f32[1,2,32,2560]{3,2,1,0:T(8,128)S(1)} %copy.24), channel_id=1, source_target_pairs={{0,1},{1,2},{2,3},{3,4},{4,5},{5,6},{6,7},{7,8},{8,9},{9,10},{10,1... | collective-permute-start | bytes 1966088 | tf_op jit(solution)/shard_map/while/body/eval_jaxpr/ppermute | solution.py:12
  94.9 12.8 %collective-permute-start = (f32[1,2,32,2560]{3,2,1,0:T(8,128)S(1)}, f32[1,2,32,2560]{3,2,1,0:T(8,128)S(1)}, u32[]{:S(2)}, u32[]{:S(2)}) collective-permute-start(f32[1,2,32,2560]{3,2,1,0:T(8,128)S(1)} %copy.24), channel_id=1, source_target_pairs={{0,1},{1,2},{2,3},{3,4},{4,5},{5,6},{6,7},{7,8},{8,9},{9,10},{10,1... | collective-permute-start | bytes 1966088 | tf_op jit(solution)/shard_map/while/body/eval_jaxpr/ppermute | solution.py:12
  107.8 12.8 %collective-permute-start = (f32[1,2,32,2560]{3,2,1,0:T(8,128)S(1)}, f32[1,2,32,2560]{3,2,1,0:T(8,128)S(1)}, u32[]{:S(2)}, u32[]{:S(2)}) collective-permute-start(f32[1,2,32,2560]{3,2,1,0:T(8,128)S(1)} %copy.24), channel_id=1, source_target_pairs={{0,1},{1,2},{2,3},{3,4},{4,5},{5,6},{6,7},{7,8},{8,9},{9,10},{10,1... | collective-permute-start | bytes 1966088 | tf_op jit(solution)/shard_map/while/body/eval_jaxpr/ppermute | solution.py:12
  120.6 12.8 %collective-permute-start = (f32[1,2,32,2560]{3,2,1,0:T(8,128)S(1)}, f32[1,2,32,2560]{3,2,1,0:T(8,128)S(1)}, u32[]{:S(2)}, u32[]{:S(2)}) collective-permute-start(f32[1,2,32,2560]{3,2,1,0:T(8,128)S(1)} %copy.24), channel_id=1, source_target_pairs={{0,1},{1,2},{2,3},{3,4},{4,5},{5,6},{6,7},{7,8},{8,9},{9,10},{10,1... | collective-permute-start | bytes 1966088 | tf_op jit(solution)/shard_map/while/body/eval_jaxpr/ppermute | solution.py:12
  133.4 12.8 %collective-permute-start = (f32[1,2,32,2560]{3,2,1,0:T(8,128)S(1)}, f32[1,2,32,2560]{3,2,1,0:T(8,128)S(1)}, u32[]{:S(2)}, u32[]{:S(2)}) collective-permute-start(f32[1,2,32,2560]{3,2,1,0:T(8,128)S(1)} %copy.24), channel_id=1, source_target_pairs={{0,1},{1,2},{2,3},{3,4},{4,5},{5,6},{6,7},{7,8},{8,9},{9,10},{10,1... | collective-permute-start | bytes 1966088 | tf_op jit(solution)/shard_map/while/body/eval_jaxpr/ppermute | solution.py:12
  146.2 12.8 %collective-permute-start = (f32[1,2,32,2560]{3,2,1,0:T(8,128)S(1)}, f32[1,2,32,2560]{3,2,1,0:T(8,128)S(1)}, u32[]{:S(2)}, u32[]{:S(2)}) collective-permute-start(f32[1,2,32,2560]{3,2,1,0:T(8,128)S(1)} %copy.24), channel_id=1, source_target_pairs={{0,1},{1,2},{2,3},{3,4},{4,5},{5,6},{6,7},{7,8},{8,9},{9,10},{10,1... | collective-permute-start | bytes 1966088 | tf_op jit(solution)/shard_map/while/body/eval_jaxpr/ppermute | solution.py:12
  159.0 12.8 %collective-permute-start = (f32[1,2,32,2560]{3,2,1,0:T(8,128)S(1)}, f32[1,2,32,2560]{3,2,1,0:T(8,128)S(1)}, u32[]{:S(2)}, u32[]{:S(2)}) collective-permute-start(f32[1,2,32,2560]{3,2,1,0:T(8,128)S(1)} %copy.24), channel_id=1, source_target_pairs={{0,1},{1,2},{2,3},{3,4},{4,5},{5,6},{6,7},{7,8},{8,9},{9,10},{10,1... | collective-permute-start | bytes 1966088 | tf_op jit(solution)/shard_map/while/body/eval_jaxpr/ppermute | solution.py:12
  171.8 12.8 %collective-permute-start = (f32[1,2,32,2560]{3,2,1,0:T(8,128)S(1)}, f32[1,2,32,2560]{3,2,1,0:T(8,128)S(1)}, u32[]{:S(2)}, u32[]{:S(2)}) collective-permute-start(f32[1,2,32,2560]{3,2,1,0:T(8,128)S(1)} %copy.24), channel_id=1, source_target_pairs={{0,1},{1,2},{2,3},{3,4},{4,5},{5,6},{6,7},{7,8},{8,9},{9,10},{10,1... | collective-permute-start | bytes 1966088 | tf_op jit(solution)/shard_map/while/body/eval_jaxpr/ppermute | solution.py:12
  184.6 12.8 %collective-permute-start = (f32[1,2,32,2560]{3,2,1,0:T(8,128)S(1)}, f32[1,2,32,2560]{3,2,1,0:T(8,128)S(1)}, u32[]{:S(2)}, u32[]{:S(2)}) collective-permute-start(f32[1,2,32,2560]{3,2,1,0:T(8,128)S(1)} %copy.24), channel_id=1, source_target_pairs={{0,1},{1,2},{2,3},{3,4},{4,5},{5,6},{6,7},{7,8},{8,9},{9,10},{10,1... | collective-permute-start | bytes 1966088 | tf_op jit(solution)/shard_map/while/body/eval_jaxpr/ppermute | solution.py:12
  197.4 12.8 %collective-permute-start = (f32[1,2,32,2560]{3,2,1,0:T(8,128)S(1)}, f32[1,2,32,2560]{3,2,1,0:T(8,128)S(1)}, u32[]{:S(2)}, u32[]{:S(2)}) collective-permute-start(f32[1,2,32,2560]{3,2,1,0:T(8,128)S(1)} %copy.24), channel_id=1, source_target_pairs={{0,1},{1,2},{2,3},{3,4},{4,5},{5,6},{6,7},{7,8},{8,9},{9,10},{10,1... | collective-permute-start | bytes 1966088 | tf_op jit(solution)/shard_map/while/body/eval_jaxpr/ppermute | solution.py:12
  210.2 12.8 %collective-permute-start = (f32[1,2,32,2560]{3,2,1,0:T(8,128)S(1)}, f32[1,2,32,2560]{3,2,1,0:T(8,128)S(1)}, u32[]{:S(2)}, u32[]{:S(2)}) collective-permute-start(f32[1,2,32,2560]{3,2,1,0:T(8,128)S(1)} %copy.24), channel_id=1, source_target_pairs={{0,1},{1,2},{2,3},{3,4},{4,5},{5,6},{6,7},{7,8},{8,9},{9,10},{10,1... | collective-permute-start | bytes 1966088 | tf_op jit(solution)/shard_map/while/body/eval_jaxpr/ppermute | solution.py:12
  223.0 12.8 %collective-permute-start = (f32[1,2,32,2560]{3,2,1,0:T(8,128)S(1)}, f32[1,2,32,2560]{3,2,1,0:T(8,128)S(1)}, u32[]{:S(2)}, u32[]{:S(2)}) collective-permute-start(f32[1,2,32,2560]{3,2,1,0:T(8,128)S(1)} %copy.24), channel_id=1, source_target_pairs={{0,1},{1,2},{2,3},{3,4},{4,5},{5,6},{6,7},{7,8},{8,9},{9,10},{10,1... | collective-permute-start | bytes 1966088 | tf_op jit(solution)/shard_map/while/body/eval_jaxpr/ppermute | solution.py:12
  235.8 12.8 %collective-permute-start = (f32[1,2,32,2560]{3,2,1,0:T(8,128)S(1)}, f32[1,2,32,2560]{3,2,1,0:T(8,128)S(1)}, u32[]{:S(2)}, u32[]{:S(2)}) collective-permute-start(f32[1,2,32,2560]{3,2,1,0:T(8,128)S(1)} %copy.24), channel_id=1, source_target_pairs={{0,1},{1,2},{2,3},{3,4},{4,5},{5,6},{6,7},{7,8},{8,9},{9,10},{10,1... | collective-permute-start | bytes 1966088 | tf_op jit(solution)/shard_map/while/body/eval_jaxpr/ppermute | solution.py:12
  248.6 12.8 %collective-permute-start = (f32[1,2,32,2560]{3,2,1,0:T(8,128)S(1)}, f32[1,2,32,2560]{3,2,1,0:T(8,128)S(1)}, u32[]{:S(2)}, u32[]{:S(2)}) collective-permute-start(f32[1,2,32,2560]{3,2,1,0:T(8,128)S(1)} %copy.24), channel_id=1, source_target_pairs={{0,1},{1,2},{2,3},{3,4},{4,5},{5,6},{6,7},{7,8},{8,9},{9,10},{10,1... | collective-permute-start | bytes 1966088 | tf_op jit(solution)/shard_map/while/body/eval_jaxpr/ppermute | solution.py:12
where the time goes:
time: 268 us; the launch traced here: 266 us
  waiting for transfers between devices  132 us (49%)
  blocking collectives  63.1 us (24%)
  matrix products  62.7 us (23%)
  other arithmetic  5.42 us (2%)
    ppermute x15, waiting for transfers between devices, passed_along(): lax.ppermute(shard, axis, [(i, (i + by) % devices) for i in range(devices)])  132 us
    psum x1, blocking collectives, local(): lax.psum((self_gram(scaled_out), self_gram(scaled_in)), 'seq')  63.1 us
    dot_general x32, matrix products, contract(): jnp.einsum('lqri,ltsi->lqrts', factors, others, precision=lax.Precision.H...  61.9 us
  transfers between devices with their start and end apart: 15, of which 15 were waited for; matrix products, arithmetic and copies ran while one was open for 22% of the time, Pallas kernels for 0%

commit v1 on v0

v1 whole, which is shorter than its diff:
```python
import functools

import jax
import jax.numpy as jnp
from jax import lax
from jax.experimental import pallas as pl
from jax.experimental.pallas import tpu as pltpu
from jax.sharding import PartitionSpec as P

damping = 0.1
epsilon = 1e-06

MESH = pl.DeviceIdType.MESH
CORES = 2
PLANE_CHIPS = 4
UP, DOWN, SIDE_UP, SIDE_DOWN = range(4)


def split(x):
    high = x.astype(jnp.bfloat16)
    low = (x - high.astype(jnp.float32)).astype(jnp.bfloat16)
    return jnp.concatenate([high, low], axis=0)


def both(*conditions):
    return functools.reduce(jnp.logical_and, conditions)


def kernel(depth, rows_y, layer_ref, seq_ids_ref, out_eigen_ref, in_eigen_ref, query_out_ref, query_in_ref,
           train_out_ref, train_in_ref, result_ref,
           held, train, total, load_sem, recv_sem, send_sem, core_sem, extra_sem):
    shards, chunks, vectors, width = held.shape
    queries = result_ref.shape[0]
    rank = vectors // queries
    train_rows, out_all = train_out_ref.shape
    out_chunks = chunks - 1
    grp = lax.axis_index("grp")
    me = lax.axis_index("seq")
    core = lax.rem(me, CORES)
    y = lax.rem(me // CORES, rows_y)
    z = me // (CORES * rows_y)
    balanced = rows_y == 2 and depth >= 4
    last = depth - 1

    def index(at_z, at_y, at_core):
        return (at_z * rows_y + at_y) * CORES + at_core

    load_out = pltpu.make_async_copy(train_out_ref, train.at[:, pl.ds(0, out_all)], load_sem.at[0])
    load_in = pltpu.make_async_copy(train_in_ref, train.at[:, pl.ds(out_all, train_in_ref.shape[1])], load_sem.at[1])
    load_out.start()
    load_in.start()

    above, below = index(z + 1, y, core), index(z - 1, y, core)
    beside, sibling = index(z, 1 - y, core), index(z, y, 1 - core)
    has_above, has_below = z < last, z > 0

    barrier = pltpu.get_barrier_semaphore()

    def greet(other):
        pl.semaphore_signal(barrier, inc=1, device_id=(grp, other), device_id_type=MESH)

    greet(sibling)
    if rows_y == 2:
        greet(beside)
    pl.when(has_above)(lambda: greet(above))
    pl.when(has_below)(lambda: greet(below))

    def send(shard, chunk, other, sem):
        pltpu.make_async_remote_copy(
            src_ref=held.at[shard, chunk], dst_ref=held.at[shard, chunk],
            send_sem=sem, recv_sem=recv_sem.at[shard, chunk],
            device_id=(grp, other), device_id_type=MESH,
        ).start()

    def arrived(shard, chunk):
        pltpu.make_async_remote_copy(
            src_ref=held.at[shard, chunk], dst_ref=held.at[shard, chunk],
            send_sem=core_sem, recv_sem=recv_sem.at[shard, chunk],
            device_id=(grp, sibling), device_id_type=MESH,
        ).wait_recv()

    def sent(block, other, sem):
        pltpu.make_async_remote_copy(
            src_ref=block, dst_ref=block, send_sem=sem, recv_sem=recv_sem.at[0, 0],
            device_id=(grp, other), device_id_type=MESH,
        ).wait_send()

    layer = layer_ref[0]

    def damped(eigen_ref, query_ref, start):
        eigen = eigen_ref[:, start:start + width]
        stored = lax.broadcasted_iota(jnp.int32, eigen.shape, 0)
        chosen = jnp.sum(jnp.where(stored == layer, eigen, 0.0), axis=0, keepdims=True)
        return query_ref[:, start:start + width] / (chosen + damping)

    for chunk in range(out_chunks):
        held[me, chunk] = damped(out_eigen_ref, query_out_ref, chunk * width)
    held[me, out_chunks] = damped(in_eigen_ref, query_in_ref, 0)

    pl.semaphore_wait(barrier, rows_y + has_above.astype(jnp.int32) + has_below.astype(jnp.int32))

    for chunk in range(chunks):
        pl.when(has_above)(lambda: send(me, chunk, above, send_sem.at[UP, 0]))
        pl.when(has_below)(lambda: send(me, chunk, below, send_sem.at[DOWN, 0]))
        if rows_y == 2:
            send(me, chunk, beside, send_sem.at[SIDE_UP, 0])
        send(me, chunk, sibling, core_sem)

    total[...] = jnp.zeros_like(total)
    load_out.wait()
    load_in.wait()

    def absorb(shard, chunk):
        kind = chunk // out_chunks
        column = jnp.where(
            chunk < out_chunks, shard * (out_chunks * width) + chunk * width, out_all + shard * width)
        mine = split(held[shard, chunk])
        theirs = split(train[:, pl.ds(pl.multiple_of(column, width), width)])
        total[kind] += lax.dot_general(
            mine, jnp.concatenate([theirs, mine], axis=0), (((1,), (1,)), ((), ())),
            preferred_element_type=jnp.float32)

    def halved(chunk, at_core):
        return chunk < (chunks + 1) // 2 - at_core * (chunks % 2)

    def crosses(to_z, from_z, chunk, at_core):
        if not balanced:
            return True
        skip = jnp.logical_or(both(to_z == 1, from_z == 0), both(to_z == last - 1, from_z == last))
        half = jnp.logical_or(both(to_z == 0, from_z == 1), both(to_z == last, from_z == last - 1))
        return jnp.logical_not(jnp.logical_or(skip, both(half, halved(chunk, at_core))))

    def arrivals(step, chunk, at_core):
        up, down = z - step, z + step
        result = [
            (up >= 0, index(up, y, at_core), UP),
            (down <= last, index(down, y, at_core), DOWN),
        ]
        if rows_y == 2:
            up, down = z - (step - 1), z + (step - 1)
            result += [
                (both(up >= 0, crosses(z, up, chunk, at_core)), index(up, 1 - y, at_core), SIDE_UP),
                (both(step > 1, down <= last, crosses(z, down, chunk, at_core)),
                 index(down, 1 - y, at_core), SIDE_DOWN),
            ]
        if balanced:
            first = jnp.logical_or(both(z == 1, step == 2), both(z == last - 1, step == 2))
            final = both(jnp.logical_or(z == 0, z == last), step == depth, halved(chunk, at_core))
            end = jnp.where(z <= 1, 1 - z, last + last - 1 - z)
            result += [(jnp.logical_or(first, final), index(end, 1 - y, at_core), None)]
        return result

    def forward(step, chunk):
        for whether, shard, kind in arrivals(step, chunk, core):
            @pl.when(whether)
            def _():
                arrived(shard, chunk)
                if kind == UP:
                    pl.when(has_above)(lambda: send(shard, chunk, above, send_sem.at[UP, step]))
                    if rows_y == 2:
                        pl.when(crosses(z, z - step, chunk, core))(
                            lambda: send(shard, chunk, beside, send_sem.at[SIDE_UP, step]))
                if kind == DOWN:
                    pl.when(has_below)(lambda: send(shard, chunk, below, send_sem.at[DOWN, step]))
                    if rows_y == 2:
                        pl.when(crosses(z, z + step, chunk, core))(
                            lambda: send(shard, chunk, beside, send_sem.at[SIDE_DOWN, step]))
                if kind == SIDE_UP and balanced:
                    pl.when(both(step == 1, z == 0))(lambda: send(shard, chunk, above, extra_sem))
                    pl.when(both(step == 1, z == last))(lambda: send(shard, chunk, below, extra_sem))
                send(shard, chunk, sibling, core_sem)
        if balanced:
            opposite = index(z, 1 - y, core)
            late = both(step == last, halved(chunk, core))
            pl.when(both(late, z == 1))(lambda: send(opposite, chunk, below, extra_sem))
            pl.when(both(late, z == last - 1))(lambda: send(opposite, chunk, above, extra_sem))

    def absorb_all(step, chunk, at_core):
        for whether, shard, _ in arrivals(step, chunk, at_core):
            @pl.when(whether)
            def _():
                if at_core is not core:
                    arrived(shard, chunk)
                absorb(shard, chunk)

    def own(chunk, _):
        absorb(me, chunk)
        return 0

    def siblings(chunk, _):
        arrived(sibling, chunk)
        absorb(sibling, chunk)
        return 0

    lax.fori_loop(0, chunks, own, 0)

    steps = depth if rows_y == 2 else depth - 1
    other_core = 1 - core

    def tick(turn, _):
        step, chunk = turn // chunks + 1, lax.rem(turn, chunks)
        forward(step, chunk)
        absorb_all(step, chunk, core)

        @pl.when(step == 1)
        def _():
            siblings(chunk, 0)

        @pl.when(turn > 0)
        def _():
            before = turn - 1
            absorb_all(before // chunks + 1, lax.rem(before, chunks), other_core)
        return 0

    lax.fori_loop(0, steps * chunks, tick, 0)
    absorb_all(steps, chunks - 1, other_core)

    sent(held.at[pl.ds(0, shards // CORES)], sibling, core_sem)

    def left(step, _):
        pl.when(both(has_above, step <= z))(lambda: sent(held.at[0], above, send_sem.at[UP, step]))
        pl.when(both(has_below, step <= last - z))(lambda: sent(held.at[0], below, send_sem.at[DOWN, step]))
        if rows_y == 2:
            for kind, from_z, some in ((SIDE_UP, z - step, z >= step),
                                       (SIDE_DOWN, z + step, both(step > 0, z + step <= last))):
                def chunk_left(chunk, _):
                    return 0
                if not balanced:
                    pl.when(some)(lambda: sent(held.at[0], beside, send_sem.at[kind, step]))
                    continue
                skip = jnp.logical_or(both(z == 1, from_z == 0), both(z == last - 1, from_z == last))
                half = jnp.logical_or(both(z == 0, from_z == 1), both(z == last, from_z == last - 1))
                pl.when(both(some, jnp.logical_not(jnp.logical_or(skip, half))))(
                    lambda: sent(held.at[0], beside, send_sem.at[kind, step]))
                for at_core in range(CORES):
                    count = chunks // 2 + at_core * (chunks % 2)
                    pl.when(both(some, half, core == at_core))(
                        lambda: sent(held.at[0, pl.ds(0, count)], beside, send_sem.at[kind, step]))
        return 0

    lax.fori_loop(0, depth, left, 0)
    if balanced:
        for other, end, near in ((above, z == 0, z == last - 1), (below, z == last, z == 1)):
            pl.when(end)(lambda: sent(held.at[0], other, extra_sem))
            for at_core in range(CORES):
                count = (chunks + 1) // 2 - at_core * (chunks % 2)
                pl.when(both(near, core == at_core))(
                    lambda: sent(held.at[0, pl.ds(0, count)], other, extra_sem))

    def whole(kind):
        rows = total[kind, :vectors] + total[kind, vectors:]
        return (rows[:, :train_rows] + rows[:, train_rows:2 * train_rows],
                rows[:, 2 * train_rows:2 * train_rows + vectors] + rows[:, 2 * train_rows + vectors:])

    cross_out, gram_out = whole(0)
    cross_in, gram_in = whole(1)
    cross = cross_out * cross_in
    gram = gram_out * gram_in
    pool = train_rows // rank
    for query in range(queries):
        lines = slice(query * rank, (query + 1) * rank)
        norm = jnp.sum(gram[lines, lines], keepdims=True)
        scale = jnp.sqrt(norm + epsilon)
        picked = jnp.zeros(seq_ids_ref.shape, jnp.float32)
        for t in range(pool):
            unscaled = jnp.sum(cross[lines, t * rank:(t + 1) * rank], keepdims=True)
            picked += jnp.where(seq_ids_ref[...] == t, unscaled, 0.0)
        result_ref[query:query + 1, :] = picked / scale


def local(rows_y, layer_ids, seq_ids, out_eigen, in_eigen, query_out, query_in, train_out, train_in):
    shards = lax.axis_size("seq")
    _, queries, rank, out_cols = query_out.shape
    in_cols = query_in.shape[3]
    vectors = queries * rank
    train_rows = train_out.shape[1] * rank
    out_all, in_all = train_out.shape[3], train_in.shape[3]
    chunks = out_cols // in_cols + 1
    depth = shards // (CORES * rows_y)
    vmem = pl.BlockSpec(memory_space=pltpu.VMEM)
    smem = pl.BlockSpec(memory_space=pltpu.SMEM)
    anywhere = pl.BlockSpec(memory_space=pl.ANY)
    return pl.pallas_call(
        functools.partial(kernel, depth, rows_y),
        out_shape=jax.ShapeDtypeStruct((queries, seq_ids.shape[0]), jnp.float32),
        in_specs=[smem, vmem, vmem, vmem, vmem, vmem, anywhere, anywhere],
        out_specs=vmem,
        scratch_shapes=[
            pltpu.VMEM((shards, chunks, vectors, in_cols), jnp.float32),
            pltpu.VMEM((train_rows, out_all + in_all), jnp.float32),
            pltpu.VMEM((2, 2 * vectors, 2 * (train_rows + vectors)), jnp.float32),
            pltpu.SemaphoreType.DMA((2,)),
            pltpu.SemaphoreType.DMA((shards, chunks)),
            pltpu.SemaphoreType.DMA((4, depth)),
            pltpu.SemaphoreType.DMA,
            pltpu.SemaphoreType.DMA,
        ],
        compiler_params=pltpu.CompilerParams(
            collective_id=0, has_side_effects=True, vmem_limit_bytes=40 * 1024 * 1024),
        name="influence",
    )(
        layer_ids,
        seq_ids.reshape(1, -1),
        out_eigen,
        in_eigen,
        query_out.reshape(vectors, out_cols),
        query_in.reshape(vectors, in_cols),
        train_out.reshape(train_rows, out_all),
        train_in.reshape(train_rows, in_all),
    )


def solution(mesh):
    in_specs = (
        P("grp"),
        P(("grp", "seq")),
        P(None, "seq"),
        P(None, "seq"),
        P(None, "grp", None, "seq"),
        P(None, "grp", None, "seq"),
        P(None, ("grp", "seq"), None, None),
        P(None, ("grp", "seq"), None, None),
    )
    out_specs = P("grp", "seq")
    rows_y = max(1, PLANE_CHIPS // mesh.shape["grp"])
    return jax.shard_map(
        functools.partial(local, rows_y), mesh=mesh, in_specs=in_specs, out_specs=out_specs, check_vma=False)
```

time: 268 us -> 70.1 us (0.26)
  waiting for transfers between devices: 132 us -> 0 us
  blocking collectives: 63.1 us -> 0 us
  matrix products: 62.7 us -> 0 us
  Pallas kernels: 0 us -> 59 us
  local copies, waits for them, and re-layouts: 0.81 us -> 9.79 us
  other arithmetic: 5.42 us -> 0 us
    ppermute x15 -> x0, waiting for transfers between devices: 132 us -> none  [passed_along(): lax.ppermute(shard, axis, [(i, (i + by) % devices) for i in range(devices)])]
    psum x1 -> x0, blocking collectives: 63.1 us -> none  [local(): lax.psum((self_gram(scaled_out), self_gram(scaled_in)), 'seq')]
    dot_general x34 -> x0, matrix products: 62.7 us -> none  [the longest x32 61.9 us: contract(): jnp.einsum('lqri,ltsi->lqrts', factors, others, precision=lax.Precision.H...]
    pallas_call x0 -> x1, Pallas kernels: none -> 59 us  [local(): pl.pallas_call(functools.partial(kernel, depth, rows_y), out_shape=jax.Sh...]
    unnamed x0 -> x15, local copies, waits for them, and re-layouts: none -> 9.79 us
  transfers between devices with their start and end apart: 15 -> 0, of which waited for: 15 -> 0; matrix products, arithmetic and copies ran while one was open for 22% -> 0% of each run, Pallas kernels for 0% -> 0%
where the time goes in v1:
time: 70.1 us; the launch traced here: 69.5 us
  Pallas kernels  59 us (84%)
  local copies, waits for them, and re-layouts  9.79 us (14%)
    pallas_call x1, Pallas kernels, local(): pl.pallas_call(functools.partial(kernel, depth, rows_y), out_shape=jax.Sh...  59 us
    unnamed x15, local copies, waits for them, and re-layouts  9.79 us

profile of v1, /device:TPU:0, one launch (start us, length us, event | category | flops | bytes accessed | tf_op | source)
XLA Modules:
  0.0 69.5 jit_solution(14864321764569525323)
XLA Ops:
  0.7 0.0 copy-start
  0.7 3.4 %copy-done = f32[1,2,32,32768]{3,2,1,0:T(8,128)S(1)} copy-done((f32[1,2,32,32768]{3,2,1,0:T(8,128)S(1)}, f32[1,2,32,32768]{3,2,1,0:T(8,128)}, u32[]{:S(2)}) %copy-start) | copy-done | bytes 8388632
  4.0 0.0 copy-start.1
  4.0 1.6 %copy-done.1 = f32[1,2,32,8192]{3,2,1,0:T(8,128)S(1)} copy-done((f32[1,2,32,8192]{3,2,1,0:T(8,128)S(1)}, f32[1,2,32,8192]{3,2,1,0:T(8,128)}, u32[]{:S(2)}) %copy-start.1) | copy-done | bytes 2097176
  5.6 0.0 copy-start.2
  5.6 1.0 %copy-done.2 = f32[1,2,32,2048]{3,2,1,0:T(8,128)S(1)} copy-done((f32[1,2,32,2048]{3,2,1,0:T(8,128)S(1)}, f32[1,2,32,2048]{3,2,1,0:T(8,128)}, u32[]{:S(2)}) %copy-start.2) | copy-done | bytes 524312
  6.7 0.0 copy-start.3
  6.7 0.9 %copy-done.3 = f32[16,2048]{1,0:T(8,128)S(1)} copy-done((f32[16,2048]{1,0:T(8,128)S(1)}, f32[16,2048]{1,0:T(8,128)}, u32[]{:S(2)}) %copy-start.3) | copy-done | bytes 131096
  7.6 0.0 copy-start.4
  7.6 0.9 %copy-done.4 = f32[1,2,32,512]{3,2,1,0:T(8,128)S(1)} copy-done((f32[1,2,32,512]{3,2,1,0:T(8,128)S(1)}, f32[1,2,32,512]{3,2,1,0:T(8,128)}, u32[]{:S(2)}) %copy-start.4) | copy-done | bytes 131096
  8.5 0.0 copy-start.5
  8.5 0.8 %copy-done.5 = f32[16,512]{1,0:T(8,128)S(1)} copy-done((f32[16,512]{1,0:T(8,128)S(1)}, f32[16,512]{1,0:T(8,128)}, u32[]{:S(2)}) %copy-start.5) | copy-done | bytes 32792
  9.2 0.0 copy-start.6
  9.2 0.7 copy-done.6
  9.9 59.0 %influence.1 = f32[2,4]{1,0:T(2,128)S(1)} custom-call(s32[1]{0:T(128)S(6)} %copy.10.layer_ref, s32[1,4]{1,0:T(1,128)S(1)} %bitcast.9, f32[16,2048]{1,0:T(8,128)S(1)} %copy-done.3, f32[16,512]{1,0:T(8,128)S(1)} %copy-done.5, f32[64,2048]{1,0:T(8,128)S(1)} %bitcast.7, f32[64,512]{1,0:T(8,128)S(1)} %bitcast.8, f32[64,32768]{1,0:T(8,128)S(1)} %bitcast.5, ...), custom_call_target="tpu_custom_call" | custom-call | tf_op jit(solution)/shard_map/influence/pallas_call | solution.py:283
  68.9 0.6 copy.11
Async XLA Ops:
  0.7 3.4 %copy-start = (f32[1,2,32,32768]{3,2,1,0:T(8,128)S(1)}, f32[1,2,32,32768]{3,2,1,0:T(8,128)}, u32[]{:S(2)}) copy-start(f32[1,2,32,32768]{3,2,1,0:T(8,128)} %param.14) | copy-start | bytes 25165828
  4.0 1.6 %copy-start.1 = (f32[1,2,32,8192]{3,2,1,0:T(8,128)S(1)}, f32[1,2,32,8192]{3,2,1,0:T(8,128)}, u32[]{:S(2)}) copy-start(f32[1,2,32,8192]{3,2,1,0:T(8,128)} %param.15) | copy-start | bytes 6291460
  5.6 1.0 %copy-start.2 = (f32[1,2,32,2048]{3,2,1,0:T(8,128)S(1)}, f32[1,2,32,2048]{3,2,1,0:T(8,128)}, u32[]{:S(2)}) copy-start(f32[1,2,32,2048]{3,2,1,0:T(8,128)} %param.12) | copy-start | bytes 1572868
  6.7 0.9 %copy-start.3 = (f32[16,2048]{1,0:T(8,128)S(1)}, f32[16,2048]{1,0:T(8,128)}, u32[]{:S(2)}) copy-start(f32[16,2048]{1,0:T(8,128)} %out_eigen_ref.1) | copy-start | bytes 393220
  7.6 0.9 %copy-start.4 = (f32[1,2,32,512]{3,2,1,0:T(8,128)S(1)}, f32[1,2,32,512]{3,2,1,0:T(8,128)}, u32[]{:S(2)}) copy-start(f32[1,2,32,512]{3,2,1,0:T(8,128)} %param.13) | copy-start | bytes 393220
  8.5 0.8 %copy-start.5 = (f32[16,512]{1,0:T(8,128)S(1)}, f32[16,512]{1,0:T(8,128)}, u32[]{:S(2)}) copy-start(f32[16,512]{1,0:T(8,128)} %in_eigen_ref.1) | copy-start | bytes 98308
  9.2 0.7 copy-start.6

commit v2 on v1

--- a/solution.py
+++ b/solution.py
@@ -26,9 +26,9 @@
     return functools.reduce(jnp.logical_and, conditions)
 
 
-def kernel(depth, rows_y, layer_ref, seq_ids_ref, out_eigen_ref, in_eigen_ref, query_out_ref, query_in_ref,
+def kernel(depth, rows_y, layer_ref, seq_ids_ref, out_eigen_hbm, in_eigen_hbm, query_out_hbm, query_in_hbm,
            train_out_ref, train_in_ref, result_ref,
-           held, train, total, load_sem, recv_sem, send_sem, core_sem, extra_sem):
+           out_eigen_ref, in_eigen_ref, query_out_ref, query_in_ref, held, train, total, load_sem, recv_sem, send_sem, core_sem, extra_sem):
     shards, chunks, vectors, width = held.shape
     queries = result_ref.shape[0]
     rank = vectors // queries
@@ -45,6 +45,14 @@
     def index(at_z, at_y, at_core):
         return (at_z * rows_y + at_y) * CORES + at_core
 
+    loads = [
+        pltpu.make_async_copy(source, target, load_sem.at[2 + place])
+        for place, (source, target) in enumerate((
+            (out_eigen_hbm, out_eigen_ref), (query_out_hbm, query_out_ref),
+            (in_eigen_hbm, in_eigen_ref), (query_in_hbm, query_in_ref)))
+    ]
+    for load in loads:
+        load.start()
     load_out = pltpu.make_async_copy(train_out_ref, train.at[:, pl.ds(0, out_all)], load_sem.at[0])
     load_in = pltpu.make_async_copy(train_in_ref, train.at[:, pl.ds(out_all, train_in_ref.shape[1])], load_sem.at[1])
     load_out.start()
@@ -93,8 +101,12 @@
         chosen = jnp.sum(jnp.where(stored == layer, eigen, 0.0), axis=0, keepdims=True)
         return query_ref[:, start:start + width] / (chosen + damping)
 
+    loads[0].wait()
+    loads[1].wait()
     for chunk in range(out_chunks):
         held[me, chunk] = damped(out_eigen_ref, query_out_ref, chunk * width)
+    loads[2].wait()
+    loads[3].wait()
     held[me, out_chunks] = damped(in_eigen_ref, query_in_ref, 0)
 
     pl.semaphore_wait(barrier, rows_y + has_above.astype(jnp.int32) + has_below.astype(jnp.int32))
@@ -279,24 +291,28 @@
     depth = shards // (CORES * rows_y)
     vmem = pl.BlockSpec(memory_space=pltpu.VMEM)
     smem = pl.BlockSpec(memory_space=pltpu.SMEM)
-    anywhere = pl.BlockSpec(memory_space=pl.ANY)
+    hbm = pl.BlockSpec(memory_space=pltpu.HBM)
     return pl.pallas_call(
         functools.partial(kernel, depth, rows_y),
         out_shape=jax.ShapeDtypeStruct((queries, seq_ids.shape[0]), jnp.float32),
-        in_specs=[smem, vmem, vmem, vmem, vmem, vmem, anywhere, anywhere],
+        in_specs=[smem, vmem, hbm, hbm, hbm, hbm, hbm, hbm],
         out_specs=vmem,
         scratch_shapes=[
+            pltpu.VMEM(out_eigen.shape, jnp.float32),
+            pltpu.VMEM(in_eigen.shape, jnp.float32),
+            pltpu.VMEM((vectors, out_cols), jnp.float32),
+            pltpu.VMEM((vectors, in_cols), jnp.float32),
             pltpu.VMEM((shards, chunks, vectors, in_cols), jnp.float32),
             pltpu.VMEM((train_rows, out_all + in_all), jnp.float32),
             pltpu.VMEM((2, 2 * vectors, 2 * (train_rows + vectors)), jnp.float32),
-            pltpu.SemaphoreType.DMA((2,)),
+            pltpu.SemaphoreType.DMA((6,)),
             pltpu.SemaphoreType.DMA((shards, chunks)),
             pltpu.SemaphoreType.DMA((4, depth)),
             pltpu.SemaphoreType.DMA,
             pltpu.SemaphoreType.DMA,
         ],
         compiler_params=pltpu.CompilerParams(
-            collective_id=0, has_side_effects=True, vmem_limit_bytes=40 * 1024 * 1024),
+            collective_id=0, has_side_effects=True, vmem_limit_bytes=63 * 1024 * 1024 + 896 * 1024),
         name="influence",
     )(
         layer_ids,

time: 70.1 us -> 61.9 us (0.88)
  local copies, waits for them, and re-layouts: 9.79 us -> 1.24 us
    unnamed x15 -> x1, local copies, waits for them, and re-layouts: 9.79 us -> 1.24 us
where the time goes in v2:
time: 61.9 us; the launch traced here: 61.5 us
  Pallas kernels  59.6 us (96%)
  local copies, waits for them, and re-layouts  1.24 us (2%)
  between operations  0.66 us (1%)
    pallas_call x1, Pallas kernels, local(): pl.pallas_call(functools.partial(kernel, depth, rows_y), out_shape=jax.Sh...  59.6 us
    unnamed x1, local copies, waits for them, and re-layouts  1.24 us

profile of v2, /device:TPU:0, one launch (start us, length us, event | category | flops | bytes accessed | tf_op | source)
XLA Modules:
  0.0 61.5 jit_solution(10599482049581757024)
XLA Ops:
  0.7 59.6 %influence.1 = f32[2,4]{1,0:T(2,128)} custom-call(s32[1]{0:T(128)S(6)} %copy.10.layer_ref, s32[1,4]{1,0:T(1,128)} %bitcast.9, f32[16,2048]{1,0:T(8,128)} %out_eigen_hbm.1, f32[16,512]{1,0:T(8,128)} %in_eigen_hbm.1, f32[64,2048]{1,0:T(8,128)} %bitcast.7, f32[64,512]{1,0:T(8,128)} %bitcast.8, f32[64,32768]{1,0:T(8,128)} %bitcast.5, f32[64,8192]{1,0:T(8,128)} %bitcast.6), custom_call_target="tpu_custom_call" | custom-call | tf_op jit(solution)/shard_map/influence/pallas_call | solution.py:295
  60.3 1.2 %copy.11 = f32[2,4]{1,0:T(2,128)} copy(f32[2,4]{1,0:T(2,128)} %influence.1) | data formatting | bytes 64

commit v3 on v2

--- a/solution.py
+++ b/solution.py
@@ -28,7 +28,9 @@
 
 def kernel(depth, rows_y, layer_ref, seq_ids_ref, out_eigen_hbm, in_eigen_hbm, query_out_hbm, query_in_hbm,
            train_out_ref, train_in_ref, result_ref,
-           out_eigen_ref, in_eigen_ref, query_out_ref, query_in_ref, held, train, total, load_sem, recv_sem, send_sem, core_sem, extra_sem):
+           out_eigen_ref, in_eigen_ref, query_out_ref, query_in_ref, held, train, total,
+           guest, guest_total, given, returned,
+           load_sem, recv_sem, send_sem, core_sem, extra_sem, guest_sem):
     shards, chunks, vectors, width = held.shape
     queries = result_ref.shape[0]
     rank = vectors // queries
@@ -41,6 +43,11 @@
     z = me // (CORES * rows_y)
     balanced = rows_y == 2 and depth >= 4
     last = depth - 1
+    lent = guest.shape[1]
+    along_z = lent + (chunks - lent) // 2
+    at_end, near_end = jnp.logical_or(z == 0, z == last), jnp.logical_or(z == 1, z == last - 1)
+    low_half = z <= 1
+    partner_z = jnp.where(low_half, 1 - z, last + last - 1 - z)
 
     def index(at_z, at_y, at_core):
         return (at_z * rows_y + at_y) * CORES + at_core
@@ -83,7 +90,7 @@
     def arrived(shard, chunk):
         pltpu.make_async_remote_copy(
             src_ref=held.at[shard, chunk], dst_ref=held.at[shard, chunk],
-            send_sem=core_sem, recv_sem=recv_sem.at[shard, chunk],
+            send_sem=core_sem.at[0], recv_sem=recv_sem.at[shard, chunk],
             device_id=(grp, sibling), device_id_type=MESH,
         ).wait_recv()
 
@@ -116,31 +123,41 @@
         pl.when(has_below)(lambda: send(me, chunk, below, send_sem.at[DOWN, 0]))
         if rows_y == 2:
             send(me, chunk, beside, send_sem.at[SIDE_UP, 0])
-        send(me, chunk, sibling, core_sem)
+        send(me, chunk, sibling, core_sem.at[0])
 
     total[...] = jnp.zeros_like(total)
+    if balanced:
+        @pl.when(jnp.logical_not(at_end))
+        def _():
+            returned[...] = jnp.zeros_like(returned)
+
     load_out.wait()
     load_in.wait()
+
+    def products(factors, others):
+        mine, theirs = split(factors), split(others)
+        return lax.dot_general(
+            mine, jnp.concatenate([theirs, mine], axis=0), (((1,), (1,)), ((), ())),
+            preferred_element_type=jnp.float32)
+
+    def folded(sums):
+        rows = sums[:vectors] + sums[vectors:]
+        return (rows[:, :train_rows] + rows[:, train_rows:2 * train_rows],
+                rows[:, 2 * train_rows:2 * train_rows + vectors] + rows[:, 2 * train_rows + vectors:])
 
     def absorb(shard, chunk):
         kind = chunk // out_chunks
         column = jnp.where(
             chunk < out_chunks, shard * (out_chunks * width) + chunk * width, out_all + shard * width)
-        mine = split(held[shard, chunk])
-        theirs = split(train[:, pl.ds(pl.multiple_of(column, width), width)])
-        total[kind] += lax.dot_general(
-            mine, jnp.concatenate([theirs, mine], axis=0), (((1,), (1,)), ((), ())),
-            preferred_element_type=jnp.float32)
-
-    def halved(chunk, at_core):
-        return chunk < (chunks + 1) // 2 - at_core * (chunks % 2)
-
-    def crosses(to_z, from_z, chunk, at_core):
+        total[kind] += products(held[shard, chunk], train[:, pl.ds(pl.multiple_of(column, width), width)])
+
+    def crosses(to_z, from_z, chunk):
         if not balanced:
             return True
         skip = jnp.logical_or(both(to_z == 1, from_z == 0), both(to_z == last - 1, from_z == last))
-        half = jnp.logical_or(both(to_z == 0, from_z == 1), both(to_z == last, from_z == last - 1))
-        return jnp.logical_not(jnp.logical_or(skip, both(half, halved(chunk, at_core))))
+        part = jnp.logical_or(both(to_z == 0, from_z == 1), both(to_z == last, from_z == last - 1))
+        outside = jnp.logical_or(chunk < lent, chunk >= along_z)
+        return jnp.logical_not(jnp.logical_or(skip, both(part, outside)))
 
     def arrivals(step, chunk, at_core):
         up, down = z - step, z + step
@@ -151,15 +168,13 @@
         if rows_y == 2:
             up, down = z - (step - 1), z + (step - 1)
             result += [
-                (both(up >= 0, crosses(z, up, chunk, at_core)), index(up, 1 - y, at_core), SIDE_UP),
-                (both(step > 1, down <= last, crosses(z, down, chunk, at_core)),
+                (both(up >= 0, crosses(z, up, chunk)), index(up, 1 - y, at_core), SIDE_UP),
+                (both(step > 1, down <= last, crosses(z, down, chunk)),
                  index(down, 1 - y, at_core), SIDE_DOWN),
             ]
         if balanced:
-            first = jnp.logical_or(both(z == 1, step == 2), both(z == last - 1, step == 2))
-            final = both(jnp.logical_or(z == 0, z == last), step == depth, halved(chunk, at_core))
-            end = jnp.where(z <= 1, 1 - z, last + last - 1 - z)
-            result += [(jnp.logical_or(first, final), index(end, 1 - y, at_core), None)]
+            along = jnp.logical_or(near_end, both(at_end, chunk >= along_z))
+            result += [(both(step == depth, along), index(partner_z, 1 - y, at_core), None)]
         return result
 
     def forward(step, chunk):
@@ -170,22 +185,53 @@
                 if kind == UP:
                     pl.when(has_above)(lambda: send(shard, chunk, above, send_sem.at[UP, step]))
                     if rows_y == 2:
-                        pl.when(crosses(z, z - step, chunk, core))(
+                        pl.when(crosses(z, z - step, chunk))(
                             lambda: send(shard, chunk, beside, send_sem.at[SIDE_UP, step]))
                 if kind == DOWN:
                     pl.when(has_below)(lambda: send(shard, chunk, below, send_sem.at[DOWN, step]))
                     if rows_y == 2:
-                        pl.when(crosses(z, z + step, chunk, core))(
+                        pl.when(crosses(z, z + step, chunk))(
                             lambda: send(shard, chunk, beside, send_sem.at[SIDE_DOWN, step]))
-                if kind == SIDE_UP and balanced:
-                    pl.when(both(step == 1, z == 0))(lambda: send(shard, chunk, above, extra_sem))
-                    pl.when(both(step == 1, z == last))(lambda: send(shard, chunk, below, extra_sem))
-                send(shard, chunk, sibling, core_sem)
+                partial = both(at_end, shard == index(partner_z, 1 - y, core)) if balanced else jnp.bool_(False)
+                send(shard, chunk, sibling, core_sem.at[partial.astype(jnp.int32)])
         if balanced:
             opposite = index(z, 1 - y, core)
-            late = both(step == last, halved(chunk, core))
-            pl.when(both(late, z == 1))(lambda: send(opposite, chunk, below, extra_sem))
-            pl.when(both(late, z == last - 1))(lambda: send(opposite, chunk, above, extra_sem))
+            for end, near, inward, outward in ((0, 1, above, below), (last, last - 1, below, above)):
+                @pl.when(both(z == end, step == 1, chunk < lent))
+                def _():
+                    for at_core in range(CORES):
+                        shard = index(near, 1 - y, at_core)
+                        column = pl.multiple_of(shard * (out_chunks * width) + chunk * width, width)
+                        pltpu.make_async_remote_copy(
+                            src_ref=train.at[:, pl.ds(column, width)], dst_ref=guest.at[at_core, chunk],
+                            send_sem=guest_sem.at[0], recv_sem=guest_sem.at[1],
+                            device_id=(grp, inward), device_id_type=MESH,
+                        ).start()
+                pl.when(both(z == end, step == 2))(lambda: send(opposite, chunk, inward, extra_sem))
+
+                @pl.when(both(z == near, step == last, chunk == 0))
+                def _():
+                    for late in range(along_z, chunks):
+                        send(opposite, late, outward, extra_sem)
+
+    def lend(sem_out, sem_in, source, target, other):
+        return pltpu.make_async_remote_copy(
+            src_ref=source, dst_ref=target, send_sem=guest_sem.at[sem_out], recv_sem=guest_sem.at[sem_in],
+            device_id=(grp, other), device_id_type=MESH)
+
+    def serve():
+        lend(0, 1, guest, guest, sibling).wait_recv()
+        guest_total[...] = jnp.zeros_like(guest_total)
+
+        def one(place, _):
+            at_core, chunk = place // lent, lax.rem(place, lent)
+            guest_total[...] += products(held[index(z, 1 - y, at_core), chunk], guest[at_core, chunk])
+            return 0
+
+        lax.fori_loop(0, CORES * lent, one, 0)
+        given[...] = jnp.concatenate(folded(guest_total[...]), axis=1)
+        pl.when(low_half)(lambda: lend(2, 3, given, returned, below).start())
+        pl.when(jnp.logical_not(low_half))(lambda: lend(2, 3, given, returned, above).start())
 
     def absorb_all(step, chunk, at_core):
         for whether, shard, _ in arrivals(step, chunk, at_core):
@@ -222,12 +268,23 @@
         def _():
             before = turn - 1
             absorb_all(before // chunks + 1, lax.rem(before, chunks), other_core)
+        if balanced:
+            pl.when(both(near_end, step == last, chunk == chunks // 2))(serve)
         return 0
 
     lax.fori_loop(0, steps * chunks, tick, 0)
     absorb_all(steps, chunks - 1, other_core)
 
-    sent(held.at[pl.ds(0, shards // CORES)], sibling, core_sem)
+    if balanced:
+        pl.when(jnp.logical_not(at_end))(
+            lambda: sent(held.at[pl.ds(0, shards // CORES)], sibling, core_sem.at[0]))
+
+        @pl.when(at_end)
+        def _():
+            sent(held.at[pl.ds(0, shards // CORES - 1)], sibling, core_sem.at[0])
+            sent(held.at[0, pl.ds(0, chunks - lent)], sibling, core_sem.at[1])
+    else:
+        sent(held.at[pl.ds(0, shards // CORES)], sibling, core_sem.at[0])
 
     def left(step, _):
         pl.when(both(has_above, step <= z))(lambda: sent(held.at[0], above, send_sem.at[UP, step]))
@@ -235,37 +292,35 @@
         if rows_y == 2:
             for kind, from_z, some in ((SIDE_UP, z - step, z >= step),
                                        (SIDE_DOWN, z + step, both(step > 0, z + step <= last))):
-                def chunk_left(chunk, _):
-                    return 0
                 if not balanced:
                     pl.when(some)(lambda: sent(held.at[0], beside, send_sem.at[kind, step]))
                     continue
                 skip = jnp.logical_or(both(z == 1, from_z == 0), both(z == last - 1, from_z == last))
-                half = jnp.logical_or(both(z == 0, from_z == 1), both(z == last, from_z == last - 1))
-                pl.when(both(some, jnp.logical_not(jnp.logical_or(skip, half))))(
+                part = jnp.logical_or(both(z == 0, from_z == 1), both(z == last, from_z == last - 1))
+                pl.when(both(some, jnp.logical_not(jnp.logical_or(skip, part))))(
                     lambda: sent(held.at[0], beside, send_sem.at[kind, step]))
-                for at_core in range(CORES):
-                    count = chunks // 2 + at_core * (chunks % 2)
-                    pl.when(both(some, half, core == at_core))(
-                        lambda: sent(held.at[0, pl.ds(0, count)], beside, send_sem.at[kind, step]))
+                pl.when(both(some, part))(
+                    lambda: sent(held.at[0, pl.ds(lent, along_z - lent)], beside, send_sem.at[kind, step]))
         return 0
 
     lax.fori_loop(0, depth, left, 0)
     if balanced:
-        for other, end, near in ((above, z == 0, z == last - 1), (below, z == last, z == 1)):
-            pl.when(end)(lambda: sent(held.at[0], other, extra_sem))
-            for at_core in range(CORES):
-                count = (chunks + 1) // 2 - at_core * (chunks % 2)
-                pl.when(both(near, core == at_core))(
-                    lambda: sent(held.at[0, pl.ds(0, count)], other, extra_sem))
-
-    def whole(kind):
-        rows = total[kind, :vectors] + total[kind, vectors:]
-        return (rows[:, :train_rows] + rows[:, train_rows:2 * train_rows],
-                rows[:, 2 * train_rows:2 * train_rows + vectors] + rows[:, 2 * train_rows + vectors:])
-
-    cross_out, gram_out = whole(0)
-    cross_in, gram_in = whole(1)
+        @pl.when(at_end)
+        def _():
+            sent(held.at[0], sibling, extra_sem)
+            lend(0, 1, guest, guest, sibling).wait_send()
+            lend(2, 3, returned, returned, sibling).wait_recv()
+
+        @pl.when(near_end)
+        def _():
+            sent(held.at[0, pl.ds(along_z, chunks - along_z)], sibling, extra_sem)
+            lend(2, 3, given, given, sibling).wait_send()
+
+    cross_out, gram_out = folded(total[0])
+    cross_in, gram_in = folded(total[1])
+    if balanced:
+        cross_out += returned[:, :train_rows]
+        gram_out += returned[:, train_rows:]
     cross = cross_out * cross_in
     gram = gram_out * gram_in
     pool = train_rows // rank
@@ -288,6 +343,7 @@
     train_rows = train_out.shape[1] * rank
     out_all, in_all = train_out.shape[3], train_in.shape[3]
     chunks = out_cols // in_cols + 1
+    lent = min(3, chunks - 2)
     depth = shards // (CORES * rows_y)
     vmem = pl.BlockSpec(memory_space=pltpu.VMEM)
     smem = pl.BlockSpec(memory_space=pltpu.SMEM)
@@ -305,11 +361,16 @@
             pltpu.VMEM((shards, chunks, vectors, in_cols), jnp.float32),
             pltpu.VMEM((train_rows, out_all + in_all), jnp.float32),
             pltpu.VMEM((2, 2 * vectors, 2 * (train_rows + vectors)), jnp.float32),
+            pltpu.VMEM((CORES, lent, train_rows, in_cols), jnp.float32),
+            pltpu.VMEM((2 * vectors, 2 * (train_rows + vectors)), jnp.float32),
+            pltpu.VMEM((vectors, train_rows + vectors), jnp.float32),
+            pltpu.VMEM((vectors, train_rows + vectors), jnp.float32),
             pltpu.SemaphoreType.DMA((6,)),
             pltpu.SemaphoreType.DMA((shards, chunks)),
             pltpu.SemaphoreType.DMA((4, depth)),
+            pltpu.SemaphoreType.DMA((2,)),
             pltpu.SemaphoreType.DMA,
-            pltpu.SemaphoreType.DMA,
+            pltpu.SemaphoreType.DMA((4,)),
         ],
         compiler_params=pltpu.CompilerParams(
             collective_id=0, has_side_effects=True, vmem_limit_bytes=63 * 1024 * 1024 + 896 * 1024),

time: 61.9 us -> 59 us (0.953)
  Pallas kernels: 59.6 us -> 57 us
    pallas_call x1, Pallas kernels: 59.6 us -> 57 us  [local(): pl.pallas_call(functools.partial(kernel, depth, rows_y), out_shape=jax.Sh...]
where the time goes in v3:
time: 59 us; the launch traced here: 58.9 us
  Pallas kernels  57 us (97%)
  local copies, waits for them, and re-layouts  1.24 us (2%)
  between operations  0.66 us (1%)
    pallas_call x1, Pallas kernels, local(): pl.pallas_call(functools.partial(kernel, depth, rows_y), out_shape=jax.Sh...  57 us
    unnamed x1, local copies, waits for them, and re-layouts  1.24 us

profile of v3, /device:TPU:0, one launch (start us, length us, event | category | flops | bytes accessed | tf_op | source)
XLA Modules:
  0.0 58.9 jit_solution(6624401963312759613)
XLA Ops:
  0.7 57.0 %influence.1 = f32[2,4]{1,0:T(2,128)} custom-call(s32[1]{0:T(128)S(6)} %copy.10.layer_ref, s32[1,4]{1,0:T(1,128)} %bitcast.9, f32[16,2048]{1,0:T(8,128)} %out_eigen_hbm.1, f32[16,512]{1,0:T(8,128)} %in_eigen_hbm.1, f32[64,2048]{1,0:T(8,128)} %bitcast.7, f32[64,512]{1,0:T(8,128)} %bitcast.8, f32[64,32768]{1,0:T(8,128)} %bitcast.5, f32[64,8192]{1,0:T(8,128)} %bitcast.6), custom_call_target="tpu_custom_call" | custom-call | tf_op jit(solution)/shard_map/influence/pallas_call | solution.py:351
  57.6 1.2 %copy.11 = f32[2,4]{1,0:T(2,128)} copy(f32[2,4]{1,0:T(2,128)} %influence.1) | data formatting | bytes 64

commit v4 on v3

--- a/solution.py
+++ b/solution.py
@@ -62,8 +62,6 @@
         load.start()
     load_out = pltpu.make_async_copy(train_out_ref, train.at[:, pl.ds(0, out_all)], load_sem.at[0])
     load_in = pltpu.make_async_copy(train_in_ref, train.at[:, pl.ds(out_all, train_in_ref.shape[1])], load_sem.at[1])
-    load_out.start()
-    load_in.start()
 
     above, below = index(z + 1, y, core), index(z - 1, y, core)
     beside, sibling = index(z, 1 - y, core), index(z, y, 1 - core)
@@ -108,22 +106,29 @@
         chosen = jnp.sum(jnp.where(stored == layer, eigen, 0.0), axis=0, keepdims=True)
         return query_ref[:, start:start + width] / (chosen + damping)
 
-    loads[0].wait()
-    loads[1].wait()
-    for chunk in range(out_chunks):
-        held[me, chunk] = damped(out_eigen_ref, query_out_ref, chunk * width)
-    loads[2].wait()
-    loads[3].wait()
-    held[me, out_chunks] = damped(in_eigen_ref, query_in_ref, 0)
-
+    for load in loads:
+        load.wait()
     pl.semaphore_wait(barrier, rows_y + has_above.astype(jnp.int32) + has_below.astype(jnp.int32))
 
+    def deferred(chunk):
+        return jnp.logical_or(both(chunk >= 1, chunk < lent), chunk >= along_z)
+
     for chunk in range(chunks):
-        pl.when(has_above)(lambda: send(me, chunk, above, send_sem.at[UP, 0]))
-        pl.when(has_below)(lambda: send(me, chunk, below, send_sem.at[DOWN, 0]))
+        if chunk < out_chunks:
+            held[me, chunk] = damped(out_eigen_ref, query_out_ref, chunk * width)
+        else:
+            held[me, chunk] = damped(in_eigen_ref, query_in_ref, 0)
+        late = balanced and (1 <= chunk < lent or chunk >= along_z)
+        pl.when(both(has_above, z != last - 1) if late else has_above)(
+            lambda: send(me, chunk, above, send_sem.at[UP, 0]))
+        pl.when(both(has_below, z != 1) if late else has_below)(
+            lambda: send(me, chunk, below, send_sem.at[DOWN, 0]))
         if rows_y == 2:
             send(me, chunk, beside, send_sem.at[SIDE_UP, 0])
         send(me, chunk, sibling, core_sem.at[0])
+
+    load_out.start()
+    load_in.start()
 
     total[...] = jnp.zeros_like(total)
     if balanced:
@@ -161,9 +166,12 @@
 
     def arrivals(step, chunk, at_core):
         up, down = z - step, z + step
+        prompt = True
+        if balanced:
+            prompt = jnp.logical_not(both(at_end, step == 1, deferred(chunk)))
         result = [
-            (up >= 0, index(up, y, at_core), UP),
-            (down <= last, index(down, y, at_core), DOWN),
+            (both(up >= 0, prompt), index(up, y, at_core), UP),
+            (both(down <= last, prompt), index(down, y, at_core), DOWN),
         ]
         if rows_y == 2:
             up, down = z - (step - 1), z + (step - 1)
@@ -174,6 +182,7 @@
             ]
         if balanced:
             along = jnp.logical_or(near_end, both(at_end, chunk >= along_z))
+            result += [(both(step == depth, at_end, deferred(chunk)), index(partner_z, y, at_core), None)]
             result += [(both(step == depth, along), index(partner_z, 1 - y, at_core), None)]
         return result
 
@@ -209,8 +218,11 @@
                         ).start()
                 pl.when(both(z == end, step == 2))(lambda: send(opposite, chunk, inward, extra_sem))
 
-                @pl.when(both(z == near, step == last, chunk == 0))
+                @pl.when(both(z == near, step == last - 1, chunk == chunks - 1))
                 def _():
+                    kind = DOWN if end == 0 else UP
+                    for late in list(range(1, lent)) + list(range(along_z, chunks)):
+                        send(me, late, outward, send_sem.at[kind, 0])
                     for late in range(along_z, chunks):
                         send(opposite, late, outward, extra_sem)
 
@@ -373,7 +385,7 @@
             pltpu.SemaphoreType.DMA((4,)),
         ],
         compiler_params=pltpu.CompilerParams(
-            collective_id=0, has_side_effects=True, vmem_limit_bytes=63 * 1024 * 1024 + 896 * 1024),
+            collective_id=0, has_side_effects=True, vmem_limit_bytes=64 * 1024 * 1024),
         name="influence",
     )(
         layer_ids,

time: 59 us -> 56.8 us (0.963)
  Pallas kernels: 57 us -> 54.8 us
    pallas_call x1, Pallas kernels: 57 us -> 54.8 us  [local(): pl.pallas_call(functools.partial(kernel, depth, rows_y), out_shape=jax.Sh...]
where the time goes in v4:
time: 56.8 us; the launch traced here: 56.7 us
  Pallas kernels  54.8 us (96%)
  local copies, waits for them, and re-layouts  1.24 us (2%)
  between operations  0.66 us (1%)
    pallas_call x1, Pallas kernels, local(): pl.pallas_call(functools.partial(kernel, depth, rows_y), out_shape=jax.Sh...  54.8 us
    unnamed x1, local copies, waits for them, and re-layouts  1.24 us

profile of v4, /device:TPU:0, one launch (start us, length us, event | category | flops | bytes accessed | tf_op | source)
XLA Modules:
  0.0 56.7 jit_solution(10105506719550439959)
XLA Ops:
  0.7 54.8 %influence.1 = f32[2,4]{1,0:T(2,128)} custom-call(s32[1]{0:T(128)S(6)} %copy.10.layer_ref, s32[1,4]{1,0:T(1,128)} %bitcast.9, f32[16,2048]{1,0:T(8,128)} %out_eigen_hbm.1, f32[16,512]{1,0:T(8,128)} %in_eigen_hbm.1, f32[64,2048]{1,0:T(8,128)} %bitcast.7, f32[64,512]{1,0:T(8,128)} %bitcast.8, f32[64,32768]{1,0:T(8,128)} %bitcast.5, f32[64,8192]{1,0:T(8,128)} %bitcast.6), custom_call_target="tpu_custom_call" | custom-call | tf_op jit(solution)/shard_map/influence/pallas_call | solution.py:363
  55.4 1.2 %copy.11 = f32[2,4]{1,0:T(2,128)} copy(f32[2,4]{1,0:T(2,128)} %influence.1) | data formatting | bytes 64

commit v5 on v4

--- a/solution.py
+++ b/solution.py
@@ -26,9 +26,9 @@
     return functools.reduce(jnp.logical_and, conditions)
 
 
-def kernel(depth, rows_y, layer_ref, seq_ids_ref, out_eigen_hbm, in_eigen_hbm, query_out_hbm, query_in_hbm,
+def kernel(depth, rows_y, layer_hbm, seq_ids_hbm, out_eigen_hbm, in_eigen_hbm, query_out_hbm, query_in_hbm,
            train_out_ref, train_in_ref, result_ref,
-           out_eigen_ref, in_eigen_ref, query_out_ref, query_in_ref, held, train, total,
+           layer_ref, seq_ids_ref, out_eigen_ref, in_eigen_ref, query_out_ref, query_in_ref, held, train, total,
            guest, guest_total, given, returned,
            load_sem, recv_sem, send_sem, core_sem, extra_sem, guest_sem):
     shards, chunks, vectors, width = held.shape
@@ -52,14 +52,6 @@
     def index(at_z, at_y, at_core):
         return (at_z * rows_y + at_y) * CORES + at_core
 
-    loads = [
-        pltpu.make_async_copy(source, target, load_sem.at[2 + place])
-        for place, (source, target) in enumerate((
-            (out_eigen_hbm, out_eigen_ref), (query_out_hbm, query_out_ref),
-            (in_eigen_hbm, in_eigen_ref), (query_in_hbm, query_in_ref)))
-    ]
-    for load in loads:
-        load.start()
     load_out = pltpu.make_async_copy(train_out_ref, train.at[:, pl.ds(0, out_all)], load_sem.at[0])
     load_in = pltpu.make_async_copy(train_in_ref, train.at[:, pl.ds(out_all, train_in_ref.shape[1])], load_sem.at[1])
 
@@ -77,6 +69,16 @@
         greet(beside)
     pl.when(has_above)(lambda: greet(above))
     pl.when(has_below)(lambda: greet(below))
+
+    loads = [
+        pltpu.make_async_copy(source, target, load_sem.at[2 + place])
+        for place, (source, target) in enumerate((
+            (out_eigen_hbm, out_eigen_ref), (query_out_hbm, query_out_ref),
+            (in_eigen_hbm, in_eigen_ref), (query_in_hbm, query_in_ref),
+            (layer_hbm, layer_ref), (seq_ids_hbm, seq_ids_ref)))
+    ]
+    for load in loads:
+        load.start()
 
     def send(shard, chunk, other, sem):
         pltpu.make_async_remote_copy(
@@ -98,12 +100,11 @@
             device_id=(grp, other), device_id_type=MESH,
         ).wait_send()
 
-    layer = layer_ref[0]
 
     def damped(eigen_ref, query_ref, start):
         eigen = eigen_ref[:, start:start + width]
         stored = lax.broadcasted_iota(jnp.int32, eigen.shape, 0)
-        chosen = jnp.sum(jnp.where(stored == layer, eigen, 0.0), axis=0, keepdims=True)
+        chosen = jnp.sum(jnp.where(stored == layer_ref[...], eigen, 0.0), axis=0, keepdims=True)
         return query_ref[:, start:start + width] / (chosen + damping)
 
     for load in loads:
@@ -269,6 +270,14 @@
 
     def tick(turn, _):
         step, chunk = turn // chunks + 1, lax.rem(turn, chunks)
+        before = turn - 1
+
+        early = both(step == steps, at_end)
+
+        def absorb_before():
+            absorb_all(before // chunks + 1, lax.rem(before, chunks), other_core)
+
+        pl.when(both(turn > 0, early))(absorb_before)
         forward(step, chunk)
         absorb_all(step, chunk, core)
 
@@ -276,10 +285,7 @@
         def _():
             siblings(chunk, 0)
 
-        @pl.when(turn > 0)
-        def _():
-            before = turn - 1
-            absorb_all(before // chunks + 1, lax.rem(before, chunks), other_core)
+        pl.when(both(turn > 0, jnp.logical_not(early)))(absorb_before)
         if balanced:
             pl.when(both(near_end, step == last, chunk == chunks // 2))(serve)
         return 0
@@ -358,14 +364,15 @@
     lent = min(3, chunks - 2)
     depth = shards // (CORES * rows_y)
     vmem = pl.BlockSpec(memory_space=pltpu.VMEM)
-    smem = pl.BlockSpec(memory_space=pltpu.SMEM)
     hbm = pl.BlockSpec(memory_space=pltpu.HBM)
     return pl.pallas_call(
         functools.partial(kernel, depth, rows_y),
         out_shape=jax.ShapeDtypeStruct((queries, seq_ids.shape[0]), jnp.float32),
-        in_specs=[smem, vmem, hbm, hbm, hbm, hbm, hbm, hbm],
+        in_specs=[hbm] * 8,
         out_specs=vmem,
         scratch_shapes=[
+            pltpu.VMEM((1, 1), jnp.int32),
+            pltpu.VMEM((1, seq_ids.shape[0]), jnp.int32),
             pltpu.VMEM(out_eigen.shape, jnp.float32),
             pltpu.VMEM(in_eigen.shape, jnp.float32),
             pltpu.VMEM((vectors, out_cols), jnp.float32),
@@ -377,7 +384,7 @@
             pltpu.VMEM((2 * vectors, 2 * (train_rows + vectors)), jnp.float32),
             pltpu.VMEM((vectors, train_rows + vectors), jnp.float32),
             pltpu.VMEM((vectors, train_rows + vectors), jnp.float32),
-            pltpu.SemaphoreType.DMA((6,)),
+            pltpu.SemaphoreType.DMA((8,)),
             pltpu.SemaphoreType.DMA((shards, chunks)),
             pltpu.SemaphoreType.DMA((4, depth)),
             pltpu.SemaphoreType.DMA((2,)),
@@ -388,7 +395,7 @@
             collective_id=0, has_side_effects=True, vmem_limit_bytes=64 * 1024 * 1024),
         name="influence",
     )(
-        layer_ids,
+        layer_ids.reshape(1, 1),
         seq_ids.reshape(1, -1),
         out_eigen,
         in_eigen,

time: 56.8 us -> 56.1 us (0.988)
  Pallas kernels: 54.8 us -> 54 us
    pallas_call x1, Pallas kernels: 54.8 us -> 54 us  [local(): pl.pallas_call(functools.partial(kernel, depth, rows_y), out_shape=jax.Sh...]
where the time goes in v5:
time: 56.1 us; the launch traced here: 55.9 us
  Pallas kernels  54 us (96%)
  local copies, waits for them, and re-layouts  1.24 us (2%)
  between operations  0.66 us (1%)
    pallas_call x1, Pallas kernels, local(): pl.pallas_call(functools.partial(kernel, depth, rows_y), out_shape=jax.Sh...  54 us
    unnamed x1, local copies, waits for them, and re-layouts  1.24 us

profile of v5, /device:TPU:0, one launch (start us, length us, event | category | flops | bytes accessed | tf_op | source)
XLA Modules:
  0.0 55.9 jit_solution(5012739469850323344)
XLA Ops:
  0.7 54.0 %influence.1 = f32[2,4]{1,0:T(2,128)} custom-call(s32[1,1]{1,0:T(1,128)} %bitcast.6.layer_hbm, s32[1,4]{1,0:T(1,128)} %bitcast.11, f32[16,2048]{1,0:T(8,128)} %out_eigen_hbm.1, f32[16,512]{1,0:T(8,128)} %in_eigen_hbm.1, f32[64,2048]{1,0:T(8,128)} %bitcast.9, f32[64,512]{1,0:T(8,128)} %bitcast.10, f32[64,32768]{1,0:T(8,128)} %bitcast.7, f32[64,8192]{1,0:T(8,128)} %bitcast.8), custom_call_target="tpu_custom_call" | custom-call | tf_op jit(solution)/shard_map/influence/pallas_call | solution.py:368
  54.7 1.2 %copy.11 = f32[2,4]{1,0:T(2,128)} copy(f32[2,4]{1,0:T(2,128)} %influence.1) | data formatting | bytes 64
